TPU v7x, 32 devices: a whole 2x2x4 slice. The times are simulated.
32 devices in a mesh: node: 4 (over y, x), grid: 8 (over z, core).
Axes of the slice: x: 2, y: 2, z: 4, core: 2. Of those that a mesh axis runs over, the one named last changes fastest.
Arguments:
- probes: float32 [1, 48, 192, 256], P(None, 'grid'), may hold values from -6 to 6
- potential: float32 [48, 192, 256], P('grid'), may hold values from -2 to 1
- warm_start: bfloat16 [4, 1, 2, 48, 192, 256], P('node', None, None, 'grid'), may hold values from -0.29882812 to 0.29882812
- shift_points: float32 [4, 2], P('node'), may hold values from -4 to 9, as said below
- quad_weights: float32 [4, 2], P('node'), may hold values from -0.3 to 0.3
Outputs:
- moments: float32 [2, 1, 2, 48, 192, 256], P(None, None, None, 'grid', 'node')
- trace_estimate: float32 [2], replicated
Inputs may be any that keep to these rules, and one draw needn't show every extreme that they name: `shift_points`: column 0 holds real parts in -1 to 9; column 1 holds imaginary parts whose magnitude lies in 1 to 4.
All inputs are finite; a program needn't handle non-finite values.
Results may differ from a plain program's by a relative error of at most 0.0003.
Values may be sent and summed in bfloat16 or wider, within the bound.
A program may use at most 192 MiB of HBM per device.

v0:
```python
import jax
import jax.numpy as jnp
from jax import lax
from jax.sharding import PartitionSpec as P

PROBES = 1
ITERS = 2
MOMENTS = 2
near_weight = 4.0 / 3.0
far_weight = -1.0 / 12.0
self_weight = -7.5


def with_halo(cells, sides, width):
    for axis, dim in sides:
        count = lax.axis_size(axis)
        head = lax.slice_in_dim(cells, 0, width, axis=dim)
        tail = lax.slice_in_dim(cells, cells.shape[dim] - width, cells.shape[dim], axis=dim)
        cells = jnp.concatenate(
            [
                lax.ppermute(tail, axis, [(i, (i + 1) % count) for i in range(count)]),
                cells,
                lax.ppermute(head, axis, [((i + 1) % count, i) for i in range(count)]),
            ],
            axis=dim,
        )
    return cells


def hamiltonian_apply(padded, potential, shift_real, shift_imag):
    middle = padded[:, :, :, 2:-2]
    near_sum = (
        padded[:, :, :, 1:-3]
        + padded[:, :, :, 3:-1]
        + (jnp.roll(middle, 1, 4) + jnp.roll(middle, -1, 4))
        + (jnp.roll(middle, 1, 5) + jnp.roll(middle, -1, 5))
    )
    far_sum = (
        padded[:, :, :, :-4]
        + padded[:, :, :, 4:]
        + (jnp.roll(middle, 2, 4) + jnp.roll(middle, -2, 4))
        + (jnp.roll(middle, 2, 5) + jnp.roll(middle, -2, 5))
    )
    laplacian = near_weight * near_sum + far_weight * far_sum + self_weight * middle
    real_shift = shift_real[:, None, None, None, None]
    imag_shift = shift_imag[:, None, None, None, None]
    real_part = middle[:, :, 0]
    imag_part = middle[:, :, 1]
    result_real = (
        real_shift * real_part
        - imag_shift * imag_part
        + 0.5 * laplacian[:, :, 0]
        - potential * real_part
    )
    result_imag = (
        real_shift * imag_part
        + imag_shift * real_part
        + 0.5 * laplacian[:, :, 1]
        - potential * imag_part
    )
    return jnp.stack([result_real, result_imag], axis=2)


def bilinear(first_vec, second_vec):
    real_sum = jnp.sum(
        first_vec[:, :, 0] * second_vec[:, :, 0] - first_vec[:, :, 1] * second_vec[:, :, 1],
        axis=(2, 3, 4),
    )
    imag_sum = jnp.sum(
        first_vec[:, :, 0] * second_vec[:, :, 1] + first_vec[:, :, 1] * second_vec[:, :, 0],
        axis=(2, 3, 4),
    )
    return jnp.stack([real_sum, imag_sum], axis=-1)


def complex_times(factor_one, factor_two):
    return jnp.stack(
        [
            factor_one[..., 0] * factor_two[..., 0] - factor_one[..., 1] * factor_two[..., 1],
            factor_one[..., 0] * factor_two[..., 1] + factor_one[..., 1] * factor_two[..., 0],
        ],
        axis=-1,
    )


def complex_divide(factor_one, factor_two):
    magnitude = factor_two[..., 0] * factor_two[..., 0] + factor_two[..., 1] * factor_two[..., 1]
    return jnp.stack(
        [
            (factor_one[..., 0] * factor_two[..., 0] + factor_one[..., 1] * factor_two[..., 1])
            / magnitude,
            (factor_one[..., 1] * factor_two[..., 0] - factor_one[..., 0] * factor_two[..., 1])
            / magnitude,
        ],
        axis=-1,
    )


def scale_field(scalars, vector):
    real_scalar = scalars[..., 0][:, :, None, None, None]
    imag_scalar = scalars[..., 1][:, :, None, None, None]
    return jnp.stack(
        [
            real_scalar * vector[:, :, 0] - imag_scalar * vector[:, :, 1],
            real_scalar * vector[:, :, 1] + imag_scalar * vector[:, :, 0],
        ],
        axis=2,
    )


def trim_planes(vector, extent_now, extent_out, along_dim):
    excess = extent_now - extent_out
    if excess == 0:
        return vector
    return lax.slice_in_dim(vector, excess, vector.shape[along_dim] - excess, axis=along_dim)


def center(vector, extent):
    return trim_planes(vector, extent, 0, 3)


def residual_norms(vector):
    return lax.psum(bilinear(vector, vector), "grid")


def per_device(probes, potential, warm_start, shift_points, quad_weights):
    shift_real = shift_points[:, 0]
    shift_imag = shift_points[:, 1]
    start_width = 2
    start_wide = with_halo(warm_start, (("grid", 3),), start_width).astype(jnp.float32)
    start_extent = start_width - 2
    solution = warm_start.astype(jnp.float32)
    potential_extent = 0
    source = jnp.stack([probes, jnp.zeros_like(probes)], axis=1)[None]
    residual = source - hamiltonian_apply(
        start_wide,
        trim_planes(potential, potential_extent, start_extent, 0),
        shift_real,
        shift_imag,
    )
    direction = residual
    extent = start_extent
    residual_extent = start_extent
    norm_now = residual_norms(center(residual, start_extent))
    for iteration in range(ITERS):
        padded = with_halo(direction, (("grid", 3),), 2)
        margin = 2
        extent_out = margin - 2
        applied = hamiltonian_apply(
            padded, trim_planes(potential, potential_extent, extent_out, 0), shift_real, shift_imag
        )
        applied, direction, extent = (
            applied,
            trim_planes(padded, margin, extent_out, 3),
            extent_out,
        )
        if iteration == 0:
            residual = direction
            residual_extent = extent
        center_part = center(direction, extent)
        curvature = lax.psum(bilinear(center_part, center(applied, extent)), "grid")
        step_length = complex_divide(norm_now, curvature)
        solution = solution + scale_field(step_length, center_part)
        residual = trim_planes(residual, residual_extent, extent, 3) - scale_field(
            step_length, applied
        )
        residual_extent = extent
        if iteration + 1 < ITERS:
            norm_next = residual_norms(center(residual, extent))
            direction = residual + scale_field(complex_divide(norm_next, norm_now), direction)
            norm_now = norm_next
    scaled_shift = jnp.stack([(shift_real - 4.0) / 5.0, shift_imag / 5.0], axis=-1)
    weight_power = quad_weights
    powers = []
    for degree in range(MOMENTS):
        powers.append(weight_power)
        weight_power = complex_times(weight_power, scaled_shift)
    coefficients = jnp.stack(powers)
    coef_real = coefficients[..., 0]
    coef_imag = coefficients[..., 1]
    highest = lax.Precision.HIGHEST
    sol_real = solution[:, :, 0]
    sol_imag = solution[:, :, 1]
    term_real = jnp.einsum("ks,spzxy->kpzxy", coef_real, sol_real, precision=highest) - jnp.einsum(
        "ks,spzxy->kpzxy", coef_imag, sol_imag, precision=highest
    )
    term_imag = jnp.einsum("ks,spzxy->kpzxy", coef_real, sol_imag, precision=highest) + jnp.einsum(
        "ks,spzxy->kpzxy", coef_imag, sol_real, precision=highest
    )
    moment_terms = jnp.stack([term_real, term_imag], axis=2)
    moments = lax.psum_scatter(moment_terms, "node", scatter_dimension=4, tiled=True)
    inner_sums = jnp.einsum("pzxy,spczxy->sc", probes, solution, precision=highest) / PROBES
    local_trace = jnp.sum(complex_times(quad_weights, inner_sums), axis=0)
    trace_estimate = lax.psum(local_trace, ("node", "grid"))
    return (moments, trace_estimate)


def solution(mesh):
    return jax.shard_map(
        per_device,
        mesh=mesh,
        in_specs=(
            P(None, "grid", None, None),
            P("grid", None, None),
            P("node", None, None, "grid", None, None),
            P("node", None),
            P("node", None),
        ),
        out_specs=(P(None, None, None, "grid", "node", None), P()),
        check_vma=False,
    )
```

profile of v0, /device:TPU:12, one launch (start us, length us, event | category | flops | bytes accessed | tf_op | source)
XLA Modules:
  0.0 308.9 jit_solution(7874606106377025501)
XLA Ops:
  15.6 2.4 collective-permute-done
  18.8 2.2 fusion.79
  22.4 2.6 fusion.78
  25.0 2.9 fusion.76
  29.8 8.3 %fusion.24 = f32[1,1,2,6,192,256]{5,4,3,2,1,0:T(8,128)} fusion(f32[1,1,2,10,192,256]{5,4,3,2,1,0:T(8,128)S(1)} %maximum_convert_fusion, f32[1,1,2,6,191,256]{5,4,3,2,1,0:T(8,128)S(1)} %get-tuple-element.31, f32[1,1,2,6,1,256]{5,4,3,2,1,0:T(1,128)S(1)} %get-tuple-element.83, f32[1,1,2,6,1,256]{5,4,3,2,1,0:T(1,128)S(1)} %get-tuple-element.82, ...), kind=kLoop, calls=%fused_computation.38 | loop fusion | flops 13565952 | bytes 33030144 | tf_op jit(solution)/shard_map/add | solution.py:44
  38.1 3.6 %fusion.54 = (f32[1,1,1,6,192,256]{5,4,3,2,1,0:T(8,128)S(1)}, f32[1,1,1,6,192,256]{5,4,3,2,1,0:T(8,128)S(1)}) fusion(f32[1,1,2,6,192,256]{5,4,3,2,1,0:T(8,128)} %fusion.24, f32[6,192,256]{2,1,0:T(8,128)S(1)} %copy-done.7, f32[1,1,2,10,192,256]{5,4,3,2,1,0:T(8,128)S(1)} %maximum_convert_fusion, f32[]{:T(128)} %bitcast.6, f32[]{:T(128)} %bitcast.4), kind=kLoop, calls=%fused_computation.97 | loop fusion | flops 4128768 | bytes 8257544 | tf_op jit(solution)/shard_map/stack | solution.py:61
  45.0 3.0 fusion.95
  52.8 1.9 pad_maximum_fusion.6
  54.7 2.6 fusion.93
  57.3 2.9 fusion.91
  60.2 3.1 %collective-permute-done.3 = f32[1,1,2,2,192,256]{5,4,3,2,1,0:T(8,128)S(1)} collective-permute-done((f32[1,1,2,2,192,256]{5,4,3,2,1,0:T(8,128)S(1)}, f32[1,1,2,2,192,256]{5,4,3,2,1,0:T(8,128)S(1)}, u32[]{:S(2)}, u32[]{:S(2)}) %collective-permute-start.3) | collective-permute-done | bytes 786464 | tf_op jit(solution)/shard_map/ppermute | solution.py:23
  63.3 10.7 %collective-permute-done.2 = f32[1,1,2,2,192,256]{5,4,3,2,1,0:T(8,128)S(1)} collective-permute-done((f32[1,1,2,2,192,256]{5,4,3,2,1,0:T(8,128)S(1)}, f32[1,1,2,2,192,256]{5,4,3,2,1,0:T(8,128)S(1)}, u32[]{:S(2)}, u32[]{:S(2)}) %collective-permute-start.2) | collective-permute-done | bytes 786464 | tf_op jit(solution)/shard_map/ppermute | solution.py:21
  74.9 9.1 %fusion.14 = f32[1,1,2,6,192,256]{5,4,3,2,1,0:T(8,128)S(1)} fusion(f32[1,1,2,6,192,256]{5,4,3,2,1,0:T(8,128)S(1)} %maximum_subtract_fusion, f32[1,1,2,2,192,256]{5,4,3,2,1,0:T(8,128)} %copy-done.23, f32[1,1,2,2,192,256]{5,4,3,2,1,0:T(8,128)} %copy-done.24, f32[1,1,2,6,191,256]{5,4,3,2,1,0:T(8,128)} %get-tuple-element.75, ...), kind=kLoop, calls=%fused_computation.23 | loop fusion | flops 15925248 | bytes 25165824 | tf_op jit(solution)/shard_map/add | solution.py:44
  84.0 4.3 %fusion.64 = (f32[]{:T(128)}, f32[]{:T(128)}, f32[6,192,256]{2,1,0:T(8,128)}, f32[6,192,256]{2,1,0:T(8,128)}) fusion(f32[1,1,2,6,192,256]{5,4,3,2,1,0:T(8,128)S(1)} %maximum_subtract_fusion, f32[6,192,256]{2,1,0:T(8,128)S(1)} %copy-done.7, f32[1,1,2,6,192,256]{5,4,3,2,1,0:T(8,128)S(1)} %fusion.14, f32[]{:T(128)} %bitcast.6, f32[]{:T(128)} %bitcast.4), kind=kLoop, calls=%fused_computation.124 | loop fusion | flops 6488062 | bytes 8257552 | tf_op jit(solution)/shard_map/reduce_sum | solution.py:65
  90.2 14.2 %all-reduce.1 = (f32[1,1,2]{2,1,0:T(1,128)S(1)}, f32[1,1,2]{2,1,0:T(1,128)S(1)}) all-reduce(f32[1,1,2]{2,1,0:T(1,128)S(1)} %copy-done.28, f32[1,1,2]{2,1,0:T(1,128)} %pad_maximum_fusion.7), channel_id=1, replica_groups=mesh['node'=4,'grid'=8] {'grid'}, use_global_device_ids=true, to_apply=%region_2.3 | all-reduce | flops 4 | bytes 32 | tf_op jit(solution)/shard_map/psum | solution.py:123
  114.1 2.1 subtract_bitcast_fusion.1
  121.4 13.6 %psum.37 = f32[1,1,2]{2,1,0:T(1,128)S(1)} all-reduce(f32[1,1,2]{2,1,0:T(1,128)S(1)} %pad_maximum_fusion.8), channel_id=1, replica_groups=mesh['node'=4,'grid'=8] {'grid'}, use_global_device_ids=true, to_apply=%region_8.9 | all-reduce | flops 2 | bytes 16 | tf_op jit(solution)/shard_map/psum | solution.py:123
  141.0 1.9 multiply_subtract_fusion.1
  145.6 3.0 fusion.86
  150.0 1.8 fusion.83
  151.9 3.6 %collective-permute-start.5 = (f32[1,1,2,2,192,256]{5,4,3,2,1,0:T(8,128)S(1)}, f32[1,1,2,2,192,256]{5,4,3,2,1,0:T(8,128)S(1)}, u32[]{:S(2)}, u32[]{:S(2)}) collective-permute-start(f32[1,1,2,2,192,256]{5,4,3,2,1,0:T(8,128)S(1)} %get-tuple-element.55), channel_id=1, source_target_pairs={{1,0},{2,1},{3,2},{4,3},{5,4},{6,5},{7,6},{0,7},{9,8},{10,9},{11,1... | collective-permute-start | bytes 2359304 | tf_op jit(solution)/shard_map/ppermute | solution.py:23
  155.4 2.6 fusion.84
  158.1 2.9 fusion.82
  161.0 12.4 %collective-permute-done.5 = f32[1,1,2,2,192,256]{5,4,3,2,1,0:T(8,128)S(1)} collective-permute-done((f32[1,1,2,2,192,256]{5,4,3,2,1,0:T(8,128)S(1)}, f32[1,1,2,2,192,256]{5,4,3,2,1,0:T(8,128)S(1)}, u32[]{:S(2)}, u32[]{:S(2)}) %collective-permute-start.5) | collective-permute-done | bytes 786464 | tf_op jit(solution)/shard_map/ppermute | solution.py:23
  175.3 9.9 %fusion.6 = f32[1,1,2,6,192,256]{5,4,3,2,1,0:T(8,128)} fusion(f32[1,1,2,6,192,256]{5,4,3,2,1,0:T(8,128)S(1)} %maximum_add_fusion.9, f32[1,1,2,2,192,256]{5,4,3,2,1,0:T(8,128)} %copy-done.25, f32[1,1,2,2,192,256]{5,4,3,2,1,0:T(8,128)} %copy-done.26, f32[1,1,2,6,191,256]{5,4,3,2,1,0:T(8,128)S(1)} %get-tuple-element.51, ...), kind=kLoop, calls=%fused_computation.15 | loop fusion | flops 15925248 | bytes 25165824 | tf_op jit(solution)/shard_map/add | solution.py:44
  185.2 3.5 %fusion.40 = (f32[6,192,256]{2,1,0:T(8,128)S(1)}, f32[6,192,256]{2,1,0:T(8,128)S(1)}) fusion(f32[1,1,2,6,192,256]{5,4,3,2,1,0:T(8,128)} %fusion.6, f32[6,192,256]{2,1,0:T(8,128)S(1)} %copy-done.8, f32[1,1,2,6,192,256]{5,4,3,2,1,0:T(8,128)S(1)} %maximum_add_fusion.9, f32[]{:T(128)} %bitcast.6, f32[]{:T(128)} %bitcast.4), kind=kLoop, calls=%fused_computation.79 | loop fusion | flops 4128768 | bytes 8257544 | tf_op jit(solution)/shard_map/sub | solution.py:50
  189.9 2.0 pad_maximum_fusion.9
  192.1 12.2 %psum.38 = f32[1,1,2]{2,1,0:T(1,128)S(1)} all-reduce(f32[1,1,2]{2,1,0:T(1,128)} %pad_maximum_fusion.9), channel_id=1, replica_groups=mesh['node'=4,'grid'=8] {'grid'}, use_global_device_ids=true, to_apply=%region_11.12 | all-reduce | flops 2 | bytes 16 | tf_op jit(solution)/shard_map/psum | solution.py:161
  216.5 2.6 pad_maximum_fusion
  220.8 2.1 fusion.108
  222.9 29.6 %fusion.68 = f32[1,2]{1,0:T(1,128)S(1)} fusion(f32[6,192,256,1]{2,1,0,3:T(8,128)S(1)} %bitcast.197, f32[2,6,192,256]{3,2,1,0:T(8,128)S(1)} %fusion.108), kind=kOutput, calls=%fused_computation.145 | convolution fusion | flops 7077888 | bytes 3538952 | tf_op jit(solution)/shard_map/pzxy,spczxy->sc/dot_general | solution.py:192
  258.1 44.0 %psum.39 = f32[2]{0:T(128)} all-reduce(f32[2]{0:T(128)S(1)} %maximum_bitcast_fusion.1), channel_id=1, replica_groups=mesh['node'=4,'grid'=8] {'node','grid'}, use_global_device_ids=true, to_apply=%region_13.14 | all-reduce | flops 2 | bytes 16 | tf_op jit(solution)/shard_map/psum | solution.py:194
  (107 shorter events, 38.7 us)
Async XLA Ops:
  7.2 10.8 %copy-start = (bf16[1,1,2,6,192,256]{5,4,3,2,1,0:T(8,128)(2,1)S(1)}, bf16[1,1,2,6,192,256]{5,4,3,2,1,0:T(8,128)(2,1)}, u32[]{:S(2)}) copy-start(bf16[1,1,2,6,192,256]{5,4,3,2,1,0:T(8,128)(2,1)} %param.7) | copy-start | bytes 3538948
  7.2 294.9 %reduce-scatter.2.cloned.1.call-start = ((), (), s32[]{:S(2)}) async-start(), calls=%async_computation.1 | async-start | bytes 5898240 | tf_op jit(solution)/shard_map/reduce_scatter | solution.py:191
  8.5 7.1 %collective-permute-start.1 = (bf16[1,1,2,2,192,256]{5,4,3,2,1,0:T(8,128)(2,1)S(1)}, bf16[1,1,2,2,192,256]{5,4,3,2,1,0:T(8,128)(2,1)S(1)}, u32[]{:S(2)}, u32[]{:S(2)}) collective-permute-start(bf16[1,1,2,2,192,256]{5,4,3,2,1,0:T(8,128)(2,1)S(1)} %get-tuple-element.85), channel_id=1, source_target_pairs={{1,0},{2,1},{3,2},{4,3},{5,4},{6,5},{7,6},{0,7},{9,8},{10,9},{11,1... | collective-permute-start | bytes 1179656 | tf_op jit(solution)/shard_map/ppermute | solution.py:23
  8.5 9.4 %collective-permute-start = (bf16[1,1,2,2,192,256]{5,4,3,2,1,0:T(8,128)(2,1)S(1)}, bf16[1,1,2,2,192,256]{5,4,3,2,1,0:T(8,128)(2,1)S(1)}, u32[]{:S(2)}, u32[]{:S(2)}) collective-permute-start(bf16[1,1,2,2,192,256]{5,4,3,2,1,0:T(8,128)(2,1)S(1)} %get-tuple-element.84), channel_id=1, source_target_pairs={{0,1},{1,2},{2,3},{3,4},{4,5},{5,6},{6,7},{7,0},{8,9},{9,10},{10,1... | collective-permute-start | bytes 1179656 | tf_op jit(solution)/shard_map/ppermute | solution.py:21
  29.8 8.3 %copy-start.7 = (f32[6,192,256]{2,1,0:T(8,128)S(1)}, f32[6,192,256]{2,1,0:T(8,128)}, u32[]{:S(2)}) copy-start(f32[6,192,256]{2,1,0:T(8,128)} %param.6) | copy-start | bytes 3538948
  38.1 3.6 %copy-start.17 = (f32[1,6,192,256]{3,2,1,0:T(8,128)S(1)}, f32[1,6,192,256]{3,2,1,0:T(8,128)}, u32[]{:S(2)}) copy-start(f32[1,6,192,256]{3,2,1,0:T(8,128)} %param.5) | copy-start | bytes 3538948
  41.7 1.4 copy-start.4
  52.3 11.0 %collective-permute-start.3 = (f32[1,1,2,2,192,256]{5,4,3,2,1,0:T(8,128)S(1)}, f32[1,1,2,2,192,256]{5,4,3,2,1,0:T(8,128)S(1)}, u32[]{:S(2)}, u32[]{:S(2)}) collective-permute-start(f32[1,1,2,2,192,256]{5,4,3,2,1,0:T(8,128)S(1)} %get-tuple-element.79), channel_id=1, source_target_pairs={{1,0},{2,1},{3,2},{4,3},{5,4},{6,5},{7,6},{0,7},{9,8},{10,9},{11,1... | collective-permute-start | bytes 2359304 | tf_op jit(solution)/shard_map/ppermute | solution.py:23
  52.3 21.7 %collective-permute-start.2 = (f32[1,1,2,2,192,256]{5,4,3,2,1,0:T(8,128)S(1)}, f32[1,1,2,2,192,256]{5,4,3,2,1,0:T(8,128)S(1)}, u32[]{:S(2)}, u32[]{:S(2)}) collective-permute-start(f32[1,1,2,2,192,256]{5,4,3,2,1,0:T(8,128)S(1)} %get-tuple-element.78), channel_id=1, source_target_pairs={{0,1},{1,2},{2,3},{3,4},{4,5},{5,6},{6,7},{7,0},{8,9},{9,10},{10,1... | collective-permute-start | bytes 2359304 | tf_op jit(solution)/shard_map/ppermute | solution.py:21
  63.3 10.7 %copy-start.23 = (f32[1,1,2,2,192,256]{5,4,3,2,1,0:T(8,128)}, f32[1,1,2,2,192,256]{5,4,3,2,1,0:T(8,128)S(1)}, u32[]{:S(2)}) copy-start(f32[1,1,2,2,192,256]{5,4,3,2,1,0:T(8,128)S(1)} %collective-permute-done.3) | copy-start | bytes 2359300
  84.0 6.2 %copy-start.28 = (f32[1,1,2]{2,1,0:T(1,128)S(1)}, f32[1,1,2]{2,1,0:T(1,128)}, u32[]{:S(2)}) copy-start(f32[1,1,2]{2,1,0:T(1,128)} %pad_maximum_fusion.6) | copy-start | bytes 28
  114.1 2.2 copy-start.2
  114.1 2.3 copy-start.5
  114.1 2.7 copy-start.18
  116.3 1.0 copy-start.9
  116.3 1.6 copy-start.11
  140.9 2.0 copy-start.3
  140.9 2.0 copy-start.6
  140.9 2.8 copy-start.10
  141.0 3.2 %copy-start.12 = (f32[1,1,1,6,192,256]{5,4,3,2,1,0:T(8,128)S(1)}, f32[1,1,1,6,192,256]{5,4,3,2,1,0:T(8,128)}, u32[]{:S(2)}) copy-start(f32[1,1,1,6,192,256]{5,4,3,2,1,0:T(8,128)} %copy-done.11) | copy-start | bytes 3538948
  141.0 3.5 %copy-start.19 = (f32[1,6,192,256]{3,2,1,0:T(8,128)S(1)}, f32[1,6,192,256]{3,2,1,0:T(8,128)}, u32[]{:S(2)}) copy-start(f32[1,6,192,256]{3,2,1,0:T(8,128)} %param.5) | copy-start | bytes 3538948
  151.9 21.5 %collective-permute-start.5 = (f32[1,1,2,2,192,256]{5,4,3,2,1,0:T(8,128)S(1)}, f32[1,1,2,2,192,256]{5,4,3,2,1,0:T(8,128)S(1)}, u32[]{:S(2)}, u32[]{:S(2)}) collective-permute-start(f32[1,1,2,2,192,256]{5,4,3,2,1,0:T(8,128)S(1)} %get-tuple-element.55), channel_id=1, source_target_pairs={{1,0},{2,1},{3,2},{4,3},{5,4},{6,5},{7,6},{0,7},{9,8},{10,9},{11,1... | collective-permute-start | bytes 2359304 | tf_op jit(solution)/shard_map/ppermute | solution.py:23
  155.4 18.9 %collective-permute-start.4 = (f32[1,1,2,2,192,256]{5,4,3,2,1,0:T(8,128)S(1)}, f32[1,1,2,2,192,256]{5,4,3,2,1,0:T(8,128)S(1)}, u32[]{:S(2)}, u32[]{:S(2)}) collective-permute-start(f32[1,1,2,2,192,256]{5,4,3,2,1,0:T(8,128)S(1)} %get-tuple-element.54), channel_id=1, source_target_pairs={{0,1},{1,2},{2,3},{3,4},{4,5},{5,6},{6,7},{7,0},{8,9},{9,10},{10,1... | collective-permute-start | bytes 2359304 | tf_op jit(solution)/shard_map/ppermute | solution.py:21
  175.3 9.9 %copy-start.8 = (f32[6,192,256]{2,1,0:T(8,128)S(1)}, f32[6,192,256]{2,1,0:T(8,128)}, u32[]{:S(2)}) copy-start(f32[6,192,256]{2,1,0:T(8,128)} %param.6) | copy-start | bytes 3538948
  188.7 3.2 %copy-start.27 = (f32[1,2]{1,0:T(1,128)S(1)}, f32[1,2]{1,0:T(1,128)}, u32[]{:S(2)}) copy-start(f32[1,2]{1,0:T(1,128)} %param.9) | copy-start | bytes 28
  212.8 1.3 copy-start.21
  212.8 2.5 copy-start.22
  213.1 2.6 copy-start.13
  213.1 2.6 copy-start.15
  219.1 1.3 copy-start.14
  219.1 1.6 copy-start.16
  220.8 2.1 copy-start.20
  (4 other events, 3.8 us)
Sparse Core Ops, SparseCore 0:
  219.3 59.3 reduce-scatter.1
where the time goes:
time: 310 us; the launch traced here: 309 us
  blocking collectives  84 us (27%)
  other arithmetic  60.8 us (20%)
  local copies, waits for them, and re-layouts  53.7 us (17%)
  between operations  46.6 us (15%)
  matrix products  29.6 us (10%)
  waiting for transfers between devices  29.5 us (10%)
  starting transfers between devices  4.66 us (2%)
    psum x1, blocking collectives, per_device(): trace_estimate = lax.psum(local_trace, ('node', 'grid'))  44 us
    dot_general x1, matrix products, per_device(): jnp.einsum('pzxy,spczxy->sc', probes, solution, precision=highest) / PROBES  29.6 us
    psum x2, blocking collectives, residual_norms(): return lax.psum(bilinear(vector, vector), 'grid')  27.8 us
    add x3, other arithmetic, hamiltonian_apply(): near_weight * near_sum + far_weight * far_sum + self_weight * middle  27.3 us
    ppermute x3, waiting for transfers between devices, with_halo(): lax.ppermute(head, axis, [((i + 1) % count, i) for i in range(count)])  15.5 us
    slice x6, local copies, waits for them, and re-layouts, hamiltonian_apply(): jnp.roll(middle, -2, 5)  14.3 us
    ppermute x3, waiting for transfers between devices, with_halo(): lax.ppermute(tail, axis, [(i, (i + 1) % count) for i in range(count)])  14 us
    slice x6, local copies, waits for them, and re-layouts, hamiltonian_apply(): jnp.roll(middle, -1, 5)  12.4 us
  transfers between devices with their start and end apart: 7, of which 5 were waited for; matrix products, arithmetic and copies ran while one was open for 16% of the time, Pallas kernels for 0%

commit v1 on v0

--- a/solution.py
+++ b/solution.py
@@ -191,7 +191,7 @@
     moments = lax.psum_scatter(moment_terms, "node", scatter_dimension=4, tiled=True)
     inner_sums = jnp.einsum("pzxy,spczxy->sc", probes, solution, precision=highest) / PROBES
     local_trace = jnp.sum(complex_times(quad_weights, inner_sums), axis=0)
-    trace_estimate = lax.psum(local_trace, ("node", "grid"))
+    trace_estimate = lax.psum(lax.psum(local_trace, "grid"), "node")
     return (moments, trace_estimate)
 
 

time: 310 us -> 294 us (0.948)
  the two profiles are of different devices: /device:TPU:12 before, /device:TPU:0 now
where the time goes in v1:
time: 294 us; the launch traced here: 293 us
  blocking collectives  70 us (24%)
  other arithmetic  60.5 us (21%)
  local copies, waits for them, and re-layouts  53.6 us (18%)
  between operations  46.3 us (16%)
  matrix products  29.6 us (10%)
  waiting for transfers between devices  27.4 us (9%)
  starting transfers between devices  5.97 us (2%)
    dot_general x1, matrix products, per_device(): jnp.einsum('pzxy,spczxy->sc', probes, solution, precision=highest) / PROBES  29.6 us
    psum x2, blocking collectives, residual_norms(): return lax.psum(bilinear(vector, vector), 'grid')  29.2 us
    add x3, other arithmetic, hamiltonian_apply(): near_weight * near_sum + far_weight * far_sum + self_weight * middle  27.3 us
    psum x2, blocking collectives, per_device(): trace_estimate = lax.psum(lax.psum(local_trace, 'grid'), 'node')  24 us
    ppermute x3, waiting for transfers between devices, with_halo(): lax.ppermute(head, axis, [((i + 1) % count, i) for i in range(count)])  21.5 us
    psum x1, blocking collectives, per_device(): curvature = lax.psum(bilinear(center_part, center(applied, extent)), 'grid')  16.9 us
    slice x6, local copies, waits for them, and re-layouts, hamiltonian_apply(): jnp.roll(middle, -2, 5)  14.2 us
    slice x6, local copies, waits for them, and re-layouts, hamiltonian_apply(): jnp.roll(middle, -1, 5)  12.5 us
  transfers between devices with their start and end apart: 7, of which 6 were waited for; matrix products, arithmetic and copies ran while one was open for 16% of the time, Pallas kernels for 0%

profile of v1, /device:TPU:0, one launch (start us, length us, event | category | flops | bytes accessed | tf_op | source)
XLA Modules:
  0.0 293.3 jit_solution(15378256440048642435)
XLA Ops:
  8.5 4.5 %collective-permute-start.1 = (bf16[1,1,2,2,192,256]{5,4,3,2,1,0:T(8,128)(2,1)S(1)}, bf16[1,1,2,2,192,256]{5,4,3,2,1,0:T(8,128)(2,1)S(1)}, u32[]{:S(2)}, u32[]{:S(2)}) collective-permute-start(bf16[1,1,2,2,192,256]{5,4,3,2,1,0:T(8,128)(2,1)S(1)} %get-tuple-element.85), channel_id=1, source_target_pairs={{1,0},{2,1},{3,2},{4,3},{5,4},{6,5},{7,6},{0,7},{9,8},{10,9},{11,1... | collective-permute-start | bytes 1179656 | tf_op jit(solution)/shard_map/ppermute | solution.py:23
  20.6 2.9 %collective-permute-done = bf16[1,1,2,2,192,256]{5,4,3,2,1,0:T(8,128)(2,1)S(1)} collective-permute-done((bf16[1,1,2,2,192,256]{5,4,3,2,1,0:T(8,128)(2,1)S(1)}, bf16[1,1,2,2,192,256]{5,4,3,2,1,0:T(8,128)(2,1)S(1)}, u32[]{:S(2)}, u32[]{:S(2)}) %collective-permute-start) | collective-permute-done | bytes 393248 | tf_op jit(solution)/shard_map/ppermute | solution.py:21
  24.4 2.2 fusion.79
  28.0 2.6 fusion.78
  30.6 2.9 fusion.76
  35.4 8.3 %fusion.24 = f32[1,1,2,6,192,256]{5,4,3,2,1,0:T(8,128)} fusion(f32[1,1,2,10,192,256]{5,4,3,2,1,0:T(8,128)S(1)} %maximum_convert_fusion, f32[1,1,2,6,191,256]{5,4,3,2,1,0:T(8,128)S(1)} %get-tuple-element.31, f32[1,1,2,6,1,256]{5,4,3,2,1,0:T(1,128)S(1)} %get-tuple-element.83, f32[1,1,2,6,1,256]{5,4,3,2,1,0:T(1,128)S(1)} %get-tuple-element.82, ...), kind=kLoop, calls=%fused_computation.38 | loop fusion | flops 13565952 | bytes 33030144 | tf_op jit(solution)/shard_map/add | solution.py:44
  43.7 3.5 %fusion.54 = (f32[1,1,1,6,192,256]{5,4,3,2,1,0:T(8,128)S(1)}, f32[1,1,1,6,192,256]{5,4,3,2,1,0:T(8,128)S(1)}) fusion(f32[1,1,2,6,192,256]{5,4,3,2,1,0:T(8,128)} %fusion.24, f32[6,192,256]{2,1,0:T(8,128)S(1)} %copy-done.7, f32[1,1,2,10,192,256]{5,4,3,2,1,0:T(8,128)S(1)} %maximum_convert_fusion, f32[]{:T(128)} %bitcast.6, f32[]{:T(128)} %bitcast.4), kind=kLoop, calls=%fused_computation.97 | loop fusion | flops 4128768 | bytes 8257544 | tf_op jit(solution)/shard_map/stack | solution.py:61
  50.5 3.0 %fusion.95 = (f32[1,1,2,6,192,255]{5,4,3,2,1,0:T(8,128)}, f32[1,1,2,6,192,255]{5,4,3,2,1,0:T(8,128)}) fusion(f32[1,1,2,6,192,256]{5,4,3,2,1,0:T(8,128)S(1)} %maximum_subtract_fusion), kind=kLoop, calls=%fused_computation.178 | loop fusion | bytes 9400320 | tf_op jit(solution)/shard_map/jit(_roll_static)/slice | solution.py:36
  58.6 1.9 pad_maximum_fusion.6
  60.5 2.6 fusion.93
  63.1 2.9 fusion.91
  66.0 9.4 %collective-permute-done.3 = f32[1,1,2,2,192,256]{5,4,3,2,1,0:T(8,128)S(1)} collective-permute-done((f32[1,1,2,2,192,256]{5,4,3,2,1,0:T(8,128)S(1)}, f32[1,1,2,2,192,256]{5,4,3,2,1,0:T(8,128)S(1)}, u32[]{:S(2)}, u32[]{:S(2)}) %collective-permute-start.3) | collective-permute-done | bytes 786464 | tf_op jit(solution)/shard_map/ppermute | solution.py:23
  75.5 2.1 collective-permute-done.2
  78.5 9.1 %fusion.14 = f32[1,1,2,6,192,256]{5,4,3,2,1,0:T(8,128)S(1)} fusion(f32[1,1,2,6,192,256]{5,4,3,2,1,0:T(8,128)S(1)} %maximum_subtract_fusion, f32[1,1,2,2,192,256]{5,4,3,2,1,0:T(8,128)} %copy-done.23, f32[1,1,2,2,192,256]{5,4,3,2,1,0:T(8,128)} %copy-done.24, f32[1,1,2,6,191,256]{5,4,3,2,1,0:T(8,128)} %get-tuple-element.75, ...), kind=kLoop, calls=%fused_computation.23 | loop fusion | flops 15925248 | bytes 25165824 | tf_op jit(solution)/shard_map/add | solution.py:44
  87.6 4.1 %fusion.64 = (f32[]{:T(128)}, f32[]{:T(128)}, f32[6,192,256]{2,1,0:T(8,128)}, f32[6,192,256]{2,1,0:T(8,128)}) fusion(f32[1,1,2,6,192,256]{5,4,3,2,1,0:T(8,128)S(1)} %maximum_subtract_fusion, f32[6,192,256]{2,1,0:T(8,128)S(1)} %copy-done.7, f32[1,1,2,6,192,256]{5,4,3,2,1,0:T(8,128)S(1)} %fusion.14, f32[]{:T(128)} %bitcast.6, f32[]{:T(128)} %bitcast.4), kind=kLoop, calls=%fused_computation.124 | loop fusion | flops 6488062 | bytes 8257552 | tf_op jit(solution)/shard_map/reduce_sum | solution.py:65
  91.8 2.0 pad_maximum_fusion.7
  93.9 15.6 %all-reduce.1 = (f32[1,1,2]{2,1,0:T(1,128)S(1)}, f32[1,1,2]{2,1,0:T(1,128)S(1)}) all-reduce(f32[1,1,2]{2,1,0:T(1,128)S(1)} %copy-done.28, f32[1,1,2]{2,1,0:T(1,128)} %pad_maximum_fusion.7), channel_id=1, replica_groups=mesh['node'=4,'grid'=8] {'grid'}, use_global_device_ids=true, to_apply=%region_2.3 | all-reduce | flops 4 | bytes 32 | tf_op jit(solution)/shard_map/psum | solution.py:123
  118.9 2.1 subtract_bitcast_fusion.1
  126.1 13.6 %psum.44 = f32[1,1,2]{2,1,0:T(1,128)S(1)} all-reduce(f32[1,1,2]{2,1,0:T(1,128)S(1)} %pad_maximum_fusion.8), channel_id=1, replica_groups=mesh['node'=4,'grid'=8] {'grid'}, use_global_device_ids=true, to_apply=%region_8.9 | all-reduce | flops 2 | bytes 16 | tf_op jit(solution)/shard_map/psum | solution.py:123
  145.5 1.9 multiply_subtract_fusion.1
  150.2 3.0 %fusion.86 = (f32[1,1,2,6,192,255]{5,4,3,2,1,0:T(8,128)}, f32[1,1,2,6,192,255]{5,4,3,2,1,0:T(8,128)}) fusion(f32[1,1,2,6,192,256]{5,4,3,2,1,0:T(8,128)S(1)} %maximum_add_fusion.9), kind=kLoop, calls=%fused_computation.169 | loop fusion | bytes 9400320 | tf_op jit(solution)/shard_map/jit(_roll_static)/slice | solution.py:36
  156.9 2.6 fusion.84
  159.6 2.9 fusion.82
  162.5 11.0 %collective-permute-done.5 = f32[1,1,2,2,192,256]{5,4,3,2,1,0:T(8,128)S(1)} collective-permute-done((f32[1,1,2,2,192,256]{5,4,3,2,1,0:T(8,128)S(1)}, f32[1,1,2,2,192,256]{5,4,3,2,1,0:T(8,128)S(1)}, u32[]{:S(2)}, u32[]{:S(2)}) %collective-permute-start.5) | collective-permute-done | bytes 786464 | tf_op jit(solution)/shard_map/ppermute | solution.py:23
  175.2 9.9 %fusion.6 = f32[1,1,2,6,192,256]{5,4,3,2,1,0:T(8,128)} fusion(f32[1,1,2,6,192,256]{5,4,3,2,1,0:T(8,128)S(1)} %maximum_add_fusion.9, f32[1,1,2,2,192,256]{5,4,3,2,1,0:T(8,128)} %copy-done.25, f32[1,1,2,2,192,256]{5,4,3,2,1,0:T(8,128)} %copy-done.26, f32[1,1,2,6,191,256]{5,4,3,2,1,0:T(8,128)S(1)} %get-tuple-element.51, ...), kind=kLoop, calls=%fused_computation.15 | loop fusion | flops 15925248 | bytes 25165824 | tf_op jit(solution)/shard_map/add | solution.py:44
  185.1 3.4 %fusion.40 = (f32[6,192,256]{2,1,0:T(8,128)S(1)}, f32[6,192,256]{2,1,0:T(8,128)S(1)}) fusion(f32[1,1,2,6,192,256]{5,4,3,2,1,0:T(8,128)} %fusion.6, f32[6,192,256]{2,1,0:T(8,128)S(1)} %copy-done.8, f32[1,1,2,6,192,256]{5,4,3,2,1,0:T(8,128)S(1)} %maximum_add_fusion.9, f32[]{:T(128)} %bitcast.6, f32[]{:T(128)} %bitcast.4), kind=kLoop, calls=%fused_computation.79 | loop fusion | flops 4128768 | bytes 8257544 | tf_op jit(solution)/shard_map/sub | solution.py:50
  191.8 16.9 %psum.45 = f32[1,1,2]{2,1,0:T(1,128)S(1)} all-reduce(f32[1,1,2]{2,1,0:T(1,128)} %pad_maximum_fusion.9), channel_id=1, replica_groups=mesh['node'=4,'grid'=8] {'grid'}, use_global_device_ids=true, to_apply=%region_11.12 | all-reduce | flops 2 | bytes 16 | tf_op jit(solution)/shard_map/psum | solution.py:161
  220.7 2.6 pad_maximum_fusion
  225.0 2.1 fusion.108
  227.1 29.6 %fusion.68 = f32[1,2]{1,0:T(1,128)S(1)} fusion(f32[6,192,256,1]{2,1,0,3:T(8,128)S(1)} %bitcast.197, f32[2,6,192,256]{3,2,1,0:T(8,128)S(1)} %fusion.108), kind=kOutput, calls=%fused_computation.145 | convolution fusion | flops 7077888 | bytes 3538952 | tf_op jit(solution)/shard_map/pzxy,spczxy->sc/dot_general | solution.py:192
  262.5 13.6 %psum.46 = f32[2]{0:T(128)S(1)} all-reduce(f32[2]{0:T(128)S(1)} %maximum_bitcast_fusion.1), channel_id=1, replica_groups=mesh['node'=4,'grid'=8] {'grid'}, use_global_device_ids=true, to_apply=%region_13.14 | all-reduce | flops 2 | bytes 16 | tf_op jit(solution)/shard_map/psum | solution.py:194
  276.1 10.4 %psum.47 = f32[2]{0:T(128)} all-reduce(f32[2]{0:T(128)S(1)} %psum.46), channel_id=1, replica_groups=mesh['node'=4,'grid'=8] {'node'}, use_global_device_ids=true, to_apply=%region_14.15 | all-reduce | flops 2 | bytes 16 | tf_op jit(solution)/shard_map/psum | solution.py:194
  (108 shorter events, 41.6 us)
Async XLA Ops:
  7.2 16.4 %copy-start = (bf16[1,1,2,6,192,256]{5,4,3,2,1,0:T(8,128)(2,1)S(1)}, bf16[1,1,2,6,192,256]{5,4,3,2,1,0:T(8,128)(2,1)}, u32[]{:S(2)}) copy-start(bf16[1,1,2,6,192,256]{5,4,3,2,1,0:T(8,128)(2,1)} %param.7) | copy-start | bytes 3538948
  7.2 279.3 %reduce-scatter.2.cloned.1.call-start = ((), (), s32[]{:S(2)}) async-start(), calls=%async_computation.1 | async-start | bytes 5898240 | tf_op jit(solution)/shard_map/reduce_scatter | solution.py:191
  8.5 12.1 %collective-permute-start.1 = (bf16[1,1,2,2,192,256]{5,4,3,2,1,0:T(8,128)(2,1)S(1)}, bf16[1,1,2,2,192,256]{5,4,3,2,1,0:T(8,128)(2,1)S(1)}, u32[]{:S(2)}, u32[]{:S(2)}) collective-permute-start(bf16[1,1,2,2,192,256]{5,4,3,2,1,0:T(8,128)(2,1)S(1)} %get-tuple-element.85), channel_id=1, source_target_pairs={{1,0},{2,1},{3,2},{4,3},{5,4},{6,5},{7,6},{0,7},{9,8},{10,9},{11,1... | collective-permute-start | bytes 1179656 | tf_op jit(solution)/shard_map/ppermute | solution.py:23
  13.0 10.5 %collective-permute-start = (bf16[1,1,2,2,192,256]{5,4,3,2,1,0:T(8,128)(2,1)S(1)}, bf16[1,1,2,2,192,256]{5,4,3,2,1,0:T(8,128)(2,1)S(1)}, u32[]{:S(2)}, u32[]{:S(2)}) collective-permute-start(bf16[1,1,2,2,192,256]{5,4,3,2,1,0:T(8,128)(2,1)S(1)} %get-tuple-element.84), channel_id=1, source_target_pairs={{0,1},{1,2},{2,3},{3,4},{4,5},{5,6},{6,7},{7,0},{8,9},{9,10},{10,1... | collective-permute-start | bytes 1179656 | tf_op jit(solution)/shard_map/ppermute | solution.py:21
  35.4 8.3 %copy-start.7 = (f32[6,192,256]{2,1,0:T(8,128)S(1)}, f32[6,192,256]{2,1,0:T(8,128)}, u32[]{:S(2)}) copy-start(f32[6,192,256]{2,1,0:T(8,128)} %param.6) | copy-start | bytes 3538948
  43.6 3.5 %copy-start.17 = (f32[1,6,192,256]{3,2,1,0:T(8,128)S(1)}, f32[1,6,192,256]{3,2,1,0:T(8,128)}, u32[]{:S(2)}) copy-start(f32[1,6,192,256]{3,2,1,0:T(8,128)} %param.5) | copy-start | bytes 3538948
  47.1 1.4 copy-start.4
  57.7 17.8 %collective-permute-start.3 = (f32[1,1,2,2,192,256]{5,4,3,2,1,0:T(8,128)S(1)}, f32[1,1,2,2,192,256]{5,4,3,2,1,0:T(8,128)S(1)}, u32[]{:S(2)}, u32[]{:S(2)}) collective-permute-start(f32[1,1,2,2,192,256]{5,4,3,2,1,0:T(8,128)S(1)} %get-tuple-element.79), channel_id=1, source_target_pairs={{1,0},{2,1},{3,2},{4,3},{5,4},{6,5},{7,6},{0,7},{9,8},{10,9},{11,1... | collective-permute-start | bytes 2359304 | tf_op jit(solution)/shard_map/ppermute | solution.py:23
  58.6 19.0 %collective-permute-start.2 = (f32[1,1,2,2,192,256]{5,4,3,2,1,0:T(8,128)S(1)}, f32[1,1,2,2,192,256]{5,4,3,2,1,0:T(8,128)S(1)}, u32[]{:S(2)}, u32[]{:S(2)}) collective-permute-start(f32[1,1,2,2,192,256]{5,4,3,2,1,0:T(8,128)S(1)} %get-tuple-element.78), channel_id=1, source_target_pairs={{0,1},{1,2},{2,3},{3,4},{4,5},{5,6},{6,7},{7,0},{8,9},{9,10},{10,1... | collective-permute-start | bytes 2359304 | tf_op jit(solution)/shard_map/ppermute | solution.py:21
  75.5 2.1 copy-start.23
  87.6 6.2 %copy-start.28 = (f32[1,1,2]{2,1,0:T(1,128)S(1)}, f32[1,1,2]{2,1,0:T(1,128)}, u32[]{:S(2)}) copy-start(f32[1,1,2]{2,1,0:T(1,128)} %pad_maximum_fusion.6) | copy-start | bytes 28
  118.9 2.2 copy-start.2
  118.9 2.3 copy-start.5
  118.9 2.7 copy-start.18
  121.0 1.0 copy-start.9
  121.0 1.6 copy-start.11
  145.5 2.0 copy-start.3
  145.5 2.0 copy-start.6
  145.5 2.8 copy-start.10
  145.5 3.2 %copy-start.12 = (f32[1,1,1,6,192,256]{5,4,3,2,1,0:T(8,128)S(1)}, f32[1,1,1,6,192,256]{5,4,3,2,1,0:T(8,128)}, u32[]{:S(2)}) copy-start(f32[1,1,1,6,192,256]{5,4,3,2,1,0:T(8,128)} %copy-done.11) | copy-start | bytes 3538948
  145.5 3.5 %copy-start.19 = (f32[1,6,192,256]{3,2,1,0:T(8,128)S(1)}, f32[1,6,192,256]{3,2,1,0:T(8,128)}, u32[]{:S(2)}) copy-start(f32[1,6,192,256]{3,2,1,0:T(8,128)} %param.5) | copy-start | bytes 3538948
  156.4 17.0 %collective-permute-start.5 = (f32[1,1,2,2,192,256]{5,4,3,2,1,0:T(8,128)S(1)}, f32[1,1,2,2,192,256]{5,4,3,2,1,0:T(8,128)S(1)}, u32[]{:S(2)}, u32[]{:S(2)}) collective-permute-start(f32[1,1,2,2,192,256]{5,4,3,2,1,0:T(8,128)S(1)} %get-tuple-element.55), channel_id=1, source_target_pairs={{1,0},{2,1},{3,2},{4,3},{5,4},{6,5},{7,6},{0,7},{9,8},{10,9},{11,1... | collective-permute-start | bytes 2359304 | tf_op jit(solution)/shard_map/ppermute | solution.py:23
  156.4 17.8 %collective-permute-start.4 = (f32[1,1,2,2,192,256]{5,4,3,2,1,0:T(8,128)S(1)}, f32[1,1,2,2,192,256]{5,4,3,2,1,0:T(8,128)S(1)}, u32[]{:S(2)}, u32[]{:S(2)}) collective-permute-start(f32[1,1,2,2,192,256]{5,4,3,2,1,0:T(8,128)S(1)} %get-tuple-element.54), channel_id=1, source_target_pairs={{0,1},{1,2},{2,3},{3,4},{4,5},{5,6},{6,7},{7,0},{8,9},{9,10},{10,1... | collective-permute-start | bytes 2359304 | tf_op jit(solution)/shard_map/ppermute | solution.py:21
  175.1 9.9 %copy-start.8 = (f32[6,192,256]{2,1,0:T(8,128)S(1)}, f32[6,192,256]{2,1,0:T(8,128)}, u32[]{:S(2)}) copy-start(f32[6,192,256]{2,1,0:T(8,128)} %param.6) | copy-start | bytes 3538948
  188.5 3.1 %copy-start.27 = (f32[1,2]{1,0:T(1,128)S(1)}, f32[1,2]{1,0:T(1,128)}, u32[]{:S(2)}) copy-start(f32[1,2]{1,0:T(1,128)} %param.9) | copy-start | bytes 28
  217.0 1.3 copy-start.21
  217.0 2.5 copy-start.22
  217.3 2.6 copy-start.13
  217.3 2.6 copy-start.15
  223.3 1.3 copy-start.14
  223.3 1.6 copy-start.16
  225.0 2.1 copy-start.20
  (4 other events, 3.7 us)
Sparse Core Ops, SparseCore 0:
  223.5 55.2 reduce-scatter.1
